TPU v7x, 512 devices: a whole 4x8x8 slice. The times are simulated.
512 devices in a mesh: pencil: 32 (over z, x_lo, core), slab: 16 (over y, x_hi).
Axes of the slice: x: 4 (x_hi: 2, x_lo: 2; x = x_hi * 2 + x_lo), y: 8, z: 8, core: 2. Of those that a mesh axis runs over, the one named last changes fastest.
Arguments:
- strain: bfloat16 [6, 16, 512, 2048], P(None, None, 'pencil', 'slab'), may hold values from -6 to 6
- labels: int32 [16, 512, 2048], P(None, 'pencil', 'slab'), may hold values from 0 to 3
- moduli: float32 [2, 4], replicated, may hold values from 0.05 to 4
Outputs:
- strain_band: float32 [6, 2, 2, 512, 2048], P(None, None, None, 'pencil', 'slab')
All inputs are finite; a program needn't handle non-finite values.
Results may differ from a plain program's by a relative error of at most 0.022.
Values may be sent and summed in bfloat16 or wider, within the bound.
A program may use at most 128 MiB of HBM per device.

v0:
```python
import math

import jax
import jax.numpy as jnp
from jax import lax
from jax.sharding import PartitionSpec as P

NX = 2048
MODES = 2
KX0 = 64
NPHASE = 4


q_floor = 0.01


def reference_medium(moduli):
    lam0 = 0.5 * (jnp.min(moduli[0]) + jnp.max(moduli[0]))
    mu0 = 0.5 * (jnp.min(moduli[1]) + jnp.max(moduli[1]))
    return (lam0, mu0)


def green(spectrum, qx, qy, qz, lam0, mu0):
    txx, tyy, tzz = (spectrum[0], spectrum[1], spectrum[2])
    tyz, txz, txy = (spectrum[3], spectrum[4], spectrum[5])
    vecx = txx * qx + txy * qy + txz * qz
    vecy = txy * qx + tyy * qy + tyz * qz
    vecz = txz * qx + tyz * qy + tzz * qz
    inner = qx * vecx + qy * vecy + qz * vecz
    square = jnp.maximum(qx * qx + qy * qy + qz * qz, q_floor)
    factor = (lam0 + mu0) / (mu0 * (lam0 + 2.0 * mu0))
    first = 1.0 / (2.0 * mu0 * square)
    second = factor * inner / (square * square)
    out_xx = -(first * (2.0 * qx * vecx) - second * qx * qx)
    out_yy = -(first * (2.0 * qy * vecy) - second * qy * qy)
    out_zz = -(first * (2.0 * qz * vecz) - second * qz * qz)
    out_yz = -(first * (qy * vecz + qz * vecy) - second * qy * qz)
    out_xz = -(first * (qx * vecz + qz * vecx) - second * qx * qz)
    out_xy = -(first * (qx * vecy + qy * vecx) - second * qx * qy)
    return jnp.stack([out_xx, out_yy, out_zz, out_yz, out_xz, out_xy], 0)


def frequencies(kx, ky, kz, size_x, size_y, size_z):
    angle_x = kx.astype(jnp.float32) * (math.pi / size_x)
    angle_y = ky.astype(jnp.float32) * (math.pi / size_y)
    angle_z = kz.astype(jnp.float32) * (math.pi / size_z)
    sin_x = jnp.sin(angle_x)[:, None, None]
    cos_x = jnp.cos(angle_x)[:, None, None]
    sin_y = jnp.sin(angle_y)[None, :, None]
    cos_y = jnp.cos(angle_y)[None, :, None]
    sin_z = jnp.sin(angle_z)[None, None, :]
    cos_z = jnp.cos(angle_z)[None, None, :]
    return (sin_x * cos_y * cos_z, cos_x * sin_y * cos_z, cos_x * cos_y * sin_z)


def split_table(full):
    high = full.astype(jnp.bfloat16)
    low = (full - high.astype(jnp.float32)).astype(jnp.bfloat16)
    return (high, low)


def twiddle(freqs, positions, length, scale):
    product = freqs[:, None] * positions[None, :] % length
    angle = product.astype(jnp.float32) * (2.0 * math.pi / length)
    cosine = jnp.cos(angle) * scale
    sine = jnp.sin(angle) * scale
    full = jnp.stack([jnp.stack([cosine, sine], 1), jnp.stack([-sine, cosine], 1)], 0)
    return split_table(full)


def along_y(tables, data):
    high, low = tables
    first = jnp.einsum("okry,crmyz->comkz", high, data, preferred_element_type=jnp.float32)
    return first + jnp.einsum("okry,crmyz->comkz", low, data, preferred_element_type=jnp.float32)


def along_last(tables, data):
    high, low = tables
    first = jnp.einsum("okrz,crmyz->comyk", high, data, preferred_element_type=jnp.float32)
    return first + jnp.einsum("okrz,crmyz->comyk", low, data, preferred_element_type=jnp.float32)


def polarize(strain, labels, moduli, lam0, mu0):
    shift_lam = jnp.zeros(labels.shape, jnp.float32)
    shift_mu = jnp.zeros(labels.shape, jnp.float32)
    for phase in range(NPHASE):
        hit = labels == phase
        shift_lam = jnp.where(hit, moduli[0, phase] - lam0, shift_lam)
        shift_mu = jnp.where(hit, moduli[1, phase] - mu0, shift_mu)
    trace = (
        strain[0].astype(jnp.float32)
        + strain[1].astype(jnp.float32)
        + strain[2].astype(jnp.float32)
    )
    comps = []
    for comp in range(6):
        values = strain[comp].astype(jnp.float32)
        if comp < 3:
            comps.append(shift_lam * trace + 2.0 * shift_mu * values)
        else:
            comps.append(2.0 * shift_mu * values)
    return jnp.stack(comps, 0).astype(jnp.bfloat16)


def per_device(strain, labels, moduli):
    planes = strain.shape[1]
    rows_y = strain.shape[2]
    rows_z = strain.shape[3]
    length_y = rows_y * lax.axis_size("pencil")
    length_z = rows_z * lax.axis_size("slab")
    lam0, mu0 = reference_medium(moduli)
    polarization = polarize(strain, labels, moduli, lam0, mu0)
    kx = KX0 + jnp.arange(MODES, dtype=jnp.int32)
    positions = jnp.arange(planes, dtype=jnp.int32)
    product = kx[:, None] * positions[None, :] % NX
    angle = product.astype(jnp.float32) * (2.0 * math.pi / NX)
    scale = 1.0 / math.sqrt(planes)
    high, low = split_table(jnp.stack([jnp.cos(angle) * scale, -jnp.sin(angle) * scale], 0))
    x_band = jnp.einsum("rmx,cxyz->crmyz", high, polarization, preferred_element_type=jnp.float32)
    x_band = (
        x_band
        + jnp.einsum("rmx,cxyz->crmyz", low, polarization, preferred_element_type=jnp.float32)
    ).astype(jnp.bfloat16)
    ky = lax.axis_index("pencil") * rows_y + jnp.arange(rows_y, dtype=jnp.int32)
    scale_y = 1.0 / math.sqrt(length_y)
    piece = lax.all_gather(x_band, "pencil", axis=3, tiled=True)
    spots = jnp.arange(piece.shape[3], dtype=jnp.int32)
    y_band = along_y(twiddle(ky, spots, length_y, scale_y), piece).astype(jnp.bfloat16)
    kz = lax.axis_index("slab") * rows_z + jnp.arange(rows_z, dtype=jnp.int32)
    scale_z = 1.0 / math.sqrt(length_z)
    piece = lax.all_gather(y_band, "slab", axis=4, tiled=True)
    spots = jnp.arange(piece.shape[4], dtype=jnp.int32)
    z_band = along_last(twiddle(kz, spots, length_z, scale_z), piece)
    qx, qy, qz = frequencies(kx, ky, kz, NX, length_y, length_z)
    return green(z_band, qx[None], qy[None], qz[None], lam0, mu0)


def solution(mesh):
    return jax.shard_map(
        per_device,
        mesh=mesh,
        in_specs=(P(None, None, "pencil", "slab"), P(None, "pencil", "slab"), P()),
        out_specs=P(None, None, None, "pencil", "slab"),
        check_vma=False,
    )
```

profile of v0, /device:TPU:1, one launch (start us, length us, event | category | flops | bytes accessed | tf_op | source)
XLA Modules:
  0.0 192.9 jit_solution(10977118161502330114)
XLA Ops:
  6.5 0.0 all-gather.3.cloned.1.call-start
  6.5 1.4 slice_reduce_fusion
  7.9 1.7 fusion.125
  12.1 1.0 fusion.124
  18.1 1.1 fusion.86
  19.2 0.1 fusion.84
  19.3 0.1 fusion.82
  19.5 0.1 cosine_multiply_fusion.2
  19.6 0.1 fusion.76
  19.7 0.1 fusion.78
  19.8 0.1 fusion.80
  19.9 0.2 fusion.58
  20.1 0.9 fusion.49
  21.0 0.0 all-gather.3.cloned.1.call-update
  21.0 0.0 all-gather.5.cloned.1.call-start
  21.1 0.2 sine_multiply_fusion.1
  21.3 74.9 %all-gather.3.cloned.1.call-done = bf16[6,2,2,512,128]{4,2,1,3,0:T(2,128)(2,1)} async-done(((bf16[6,2,2,16,128]{4,2,1,3,0:T(2,128)(2,1)}), bf16[6,2,2,512,128]{4,2,1,3,0:T(2,128)(2,1)}) %all-gather.3.cloned.1.call-update) | async-done | bytes 3145744 | tf_op jit(solution)/shard_map/all_gather | solution.py:126
  96.2 0.0 copy-start.2
  96.2 2.7 %fusion.23 = f32[6,2,128,2,16]{2,4,3,1,0:T(8,128)S(1)} fusion(bf16[6,2,2,512,128,1]{4,2,1,3,0,5:T(2,128)(2,1)} %bitcast.184, f32[1,16,2,512]{3,1,2,0:T(8,128)S(1)} %get-tuple-element.28, f32[1,16,2,512]{3,1,2,0:T(8,128)S(1)} %get-tuple-element.27), kind=kOutput, calls=%fused_computation.21 | convolution fusion | flops 100794368 | bytes 3473408 | tf_op jit(solution)/shard_map/okry,crmyz->comkz/dot_general | solution.py:73
  98.9 0.2 copy-done.2
  99.0 1.3 fusion.46
  100.3 0.0 all-gather.5.cloned.1.call-update
  100.5 0.1 broadcast_multiply_fusion.3
  100.6 0.1 fusion.98
  100.7 4.2 %sine_multiply_fusion = (f32[128,1,2048]{2,0,1:T(8,128)S(1)}, f32[128,1,2048]{2,0,1:T(8,128)S(1)}, f32[128,1,2048]{2,0,1:T(8,128)S(1)}) fusion(s32[128]{0:T(128)S(1)} %iota_add_fusion), kind=kLoop, calls=%fused_computation.33 | loop fusion | flops 4456448 | bytes 3146240 | tf_op jit(solution)/shard_map/mul | solution.py:66
  105.0 1.8 maximum_bitcast_fusion
  106.8 74.3 %all-gather.5.cloned.1.call-done = bf16[6,2,2,16,2048]{4,3,1,2,0:T(8,128)(2,1)} async-done(((bf16[6,2,2,16,128]{4,3,1,2,0:T(8,128)(2,1)}), bf16[6,2,2,16,2048]{4,3,1,2,0:T(8,128)(2,1)}) %all-gather.5.cloned.1.call-update) | async-done | bytes 1572880 | tf_op jit(solution)/shard_map/all_gather | solution.py:131
  181.1 0.0 copy-start
  181.1 0.0 copy-start.1
  181.1 3.1 %fusion.13 = f32[6,2,16,2,128]{4,2,3,1,0:T(8,128)S(1)} fusion(f32[1,128,2,2048]{3,1,2,0:T(8,128)} %get-tuple-element.20, f32[1,128,2,2048]{3,1,2,0:T(8,128)S(1)} %get-tuple-element.19, bf16[6,2,2,16,2048]{4,3,1,2,0:T(8,128)(2,1)} %all-gather.5.cloned.1.call-done), kind=kOutput, calls=%fused_computation.19 | convolution fusion | flops 407896064 | bytes 5963776 | tf_op jit(solution)/shard_map/okrz,crmyz->comyk/dot_general | solution.py:80
  184.2 0.0 copy-done
  184.2 0.1 copy-done.1
  184.2 0.9 fusion.37
  185.1 0.1 negate_dynamic-update-slice_fusion.5
  185.3 0.7 copy.16
  (12 shorter events, 0.2 us)
Async XLA Ops:
  6.5 89.7 %all-gather.3.cloned.1.call-start = ((), (), s32[]{:S(2)}) async-start(), calls=%async_computation | async-start | bytes 3244032 | tf_op jit(solution)/shard_map/all_gather | solution.py:126
  21.0 160.1 %all-gather.5.cloned.1.call-start = ((), (), s32[]{:S(2)}) async-start(), calls=%async_computation.1 | async-start | bytes 1671168 | tf_op jit(solution)/shard_map/all_gather | solution.py:131
  96.2 2.8 %copy-start.2 = (bf16[6,2,2,512,128]{4,2,1,3,0:T(2,128)(2,1)S(1)}, bf16[6,2,2,512,128]{4,2,1,3,0:T(2,128)(2,1)}, u32[]{:S(2)}) copy-start(bf16[6,2,2,512,128]{4,2,1,3,0:T(2,128)(2,1)} %all-gather.3.cloned.1.call-done) | copy-start | bytes 9437188
  181.1 3.1 %copy-start = (f32[1,128,2,2048]{3,1,2,0:T(8,128)S(1)}, f32[1,128,2,2048]{3,1,2,0:T(8,128)}, u32[]{:S(2)}) copy-start(f32[1,128,2,2048]{3,1,2,0:T(8,128)} %get-tuple-element.20) | copy-start | bytes 6291460
  181.1 3.1 %copy-start.1 = (bf16[6,2,2,16,2048]{4,3,1,2,0:T(8,128)(2,1)S(1)}, bf16[6,2,2,16,2048]{4,3,1,2,0:T(8,128)(2,1)}, u32[]{:S(2)}) copy-start(bf16[6,2,2,16,2048]{4,3,1,2,0:T(8,128)(2,1)} %all-gather.5.cloned.1.call-done) | copy-start | bytes 4718596
Sparse Core Ops, SparseCore 0:
  21.2 75.0 all-gather.2
  100.5 80.6 all-gather.4
where the time goes:
time: 196 us; the launch traced here: 193 us
  waiting for transfers between devices  149 us (76%)
  between operations  21.1 us (11%)
  other arithmetic  9.92 us (5%)
  matrix products  9 us (5%)
  local copies, waits for them, and re-layouts  3.62 us (2%)
    all_gather x1, waiting for transfers between devices, per_device(): piece = lax.all_gather(x_band, 'pencil', axis=3, tiled=True)  74.9 us
    all_gather x1, waiting for transfers between devices, per_device(): piece = lax.all_gather(y_band, 'slab', axis=4, tiled=True)  74.3 us
    mul x2, other arithmetic, twiddle(): sine = jnp.sin(angle) * scale  4.45 us
  transfers between devices with their start and end apart: 2, of which 2 were waited for; matrix products, arithmetic and copies ran while one was open for 3% of the time, Pallas kernels for 0%

commit v1 on v0

v1 whole, which is shorter than its diff:
```python
import math

import jax
import jax.numpy as jnp
import numpy as np
from jax import lax
from jax.experimental import pallas as pl
from jax.experimental.pallas import tpu as pltpu
from jax.sharding import PartitionSpec as P

MESH = pl.DeviceIdType.MESH
NX, NY, NZ = 2048, 512, 2048
XW, MODES, KX0, NPHASE, COMPS = 16, 2, 64, 4, 6
PENCIL, SLAB = 32, 16
UNITS_Y, UNITS_Z = 24, 12
Q_FLOOR = 0.01
F32, BF16 = jnp.float32, jnp.bfloat16


def unit_place(unit):
    return unit // 3 * 4 + unit % 3


def place_unit(place):
    return place // 4 * 3 + place % 4


def tables():
    angle = 2 * math.pi / NY * (np.outer(np.arange(NY), np.arange(NY)) % NY)
    along_y = np.concatenate([np.cos(angle), np.sin(angle)], 1)
    angle = 2 * math.pi / 32 * (np.outer(np.arange(32), np.arange(32)) % 32)
    same = np.eye(16)
    coarse = [np.einsum("bt,kj->kbtj", f(angle), same).reshape(512, 512) for f in (np.cos, np.sin)]
    coarse = np.concatenate(coarse, 1)
    angle = 2 * math.pi / NZ * np.outer(np.arange(32), np.arange(64))
    scale = 1 / math.sqrt(NZ)
    turn = np.stack([np.tile(np.cos(angle), 2), np.concatenate([np.sin(angle), -np.sin(angle)], 1)]) * scale
    angle = 2 * math.pi / 64 * (np.outer(np.arange(64), np.arange(64)) % 64)
    cosine, sine = np.cos(angle), np.sin(angle)
    fine = np.stack([np.concatenate([cosine, sine], 1), np.concatenate([-sine, cosine], 1)])
    fine = fine.reshape(2, 16, 4, 128).transpose(1, 0, 2, 3)
    fine = np.stack([np.roll(fine, -delta, 2).reshape(128, 128) for delta in range(4)])
    rows = np.arange(32)
    ky = 16 * np.arange(PENCIL)[:, None] + (rows // 8 * 4 + rows % 4)[None, :]
    angle = np.broadcast_to((math.pi / NY * ky)[:, :, None], (PENCIL, 32, 128))
    freq_y = np.stack([np.sin(angle), np.cos(angle)], 1)
    angle = math.pi / NZ * np.arange(NZ).reshape(SLAB, 1, 128)
    angle = np.broadcast_to(angle, (SLAB, 8, 128))
    freq_z = np.stack([np.sin(angle), np.cos(angle)], 1)
    return (
        along_y.astype(BF16),
        coarse.astype(BF16),
        turn.astype(np.float32),
        fine.astype(BF16),
        freq_y.astype(np.float32),
        freq_z.astype(np.float32),
    )


def swap_parts(values):
    lane = lax.broadcasted_iota(jnp.int32, values.shape, 1)
    turned = pltpu.roll(values, 64, 1)
    return jnp.where(lane < 64, turned, -turned)


def with_swapped(tile):
    return jnp.concatenate([tile, swap_parts(tile.astype(F32)).astype(BF16)], 0)


def transform_z(data, coarse, turn, fine):
    mixed = jnp.dot(coarse, with_swapped(data), preferred_element_type=F32)
    swapped = pltpu.roll(mixed, 64, 1)
    mixed = mixed.reshape(16, 32, 128) * turn[0][None] + swapped.reshape(16, 32, 128) * turn[1][None]
    mixed = mixed.reshape(512, 128).astype(BF16)
    blocks = [mixed[32 * k : 32 * k + 32] for k in range(16)]
    row = lax.broadcasted_iota(jnp.int32, (128, 512), 0)
    lane = lax.broadcasted_iota(jnp.int32, (128, 512), 1)
    shift = (lane // 32 - row) & 3
    result = None
    for delta in range(4):
        turned = jnp.concatenate([blocks[4 * (k // 4) + (k - delta) % 4] for k in range(16)], 0)
        part = lax.dot_general(fine[delta], turned, (((1,), (1,)), ((), ())), preferred_element_type=F32)
        result = part if result is None else jnp.where(shift == delta, part, result)
    return result


def contrast(labels, values, base, factor):
    levels = [(values[phase] - base) * factor for phase in range(NPHASE)]
    chosen = jnp.where(labels == 2, levels[2], levels[3])
    chosen = jnp.where(labels == 1, levels[1], chosen)
    return jnp.where(labels == 0, levels[0], chosen)


def wave(mode, plane):
    angle = 2 * math.pi / NX * ((KX0 + mode) * plane % NX)
    scale = 1 / math.sqrt(XW)
    return float(math.cos(angle) * scale), float(-math.sin(angle) * scale)


def kernel(
    moduli,
    strain_hbm,
    labels_hbm,
    along_y_hbm,
    coarse_hbm,
    turn_hbm,
    fine_hbm,
    freq_y_hbm,
    freq_z_hbm,
    out,
    strain,
    labels,
    along_y,
    coarse,
    turn,
    fine,
    freq_y,
    freq_z,
    shear,
    send1,
    land1,
    send2,
    land2,
    send3,
    land3,
    in_sems,
    table_sems,
    send_sems,
    land_sems,
):
    pencil = lax.axis_index("pencil")
    slab = lax.axis_index("slab")
    works_y = pencil % 4 < 3
    works_z = slab % 4 < 3

    loads = [
        pltpu.make_async_copy(strain_hbm, strain, in_sems.at[0]),
        pltpu.make_async_copy(labels_hbm, labels, in_sems.at[1]),
    ]
    for load in loads:
        load.start()
    pairs = [
        (freq_y_hbm.at[pencil], freq_y),
        (freq_z_hbm.at[slab], freq_z),
        (along_y_hbm, along_y),
        (coarse_hbm, coarse),
        (turn_hbm, turn),
        (fine_hbm, fine),
    ]
    table_loads = [pltpu.make_async_copy(a, b, table_sems.at[i]) for i, (a, b) in enumerate(pairs)]
    for load in table_loads:
        load.start()

    barrier = pltpu.get_barrier_semaphore()

    @pl.when(works_y)
    def _():
        def greet(step, carry):
            other = lax.rem(pencil + step, PENCIL)
            pl.semaphore_signal(barrier, inc=1, device_id=(other, slab), device_id_type=MESH)
            return carry

        lax.fori_loop(1, PENCIL, greet, 0)

    @pl.when(works_z)
    def _():
        def greet(step, carry):
            other = lax.rem(slab + step, SLAB)
            pl.semaphore_signal(barrier, inc=1, device_id=(pencil, other), device_id_type=MESH)
            return carry

        lax.fori_loop(1, SLAB, greet, 0)

    lam0 = 0.5 * (
        jnp.minimum(jnp.minimum(moduli[0, 0], moduli[0, 1]), jnp.minimum(moduli[0, 2], moduli[0, 3]))
        + jnp.maximum(jnp.maximum(moduli[0, 0], moduli[0, 1]), jnp.maximum(moduli[0, 2], moduli[0, 3]))
    )
    mu0 = 0.5 * (
        jnp.minimum(jnp.minimum(moduli[1, 0], moduli[1, 1]), jnp.minimum(moduli[1, 2], moduli[1, 3]))
        + jnp.maximum(jnp.maximum(moduli[1, 0], moduli[1, 1]), jnp.maximum(moduli[1, 2], moduli[1, 3]))
    )

    for load in loads:
        load.wait()
    lane = lax.broadcasted_iota(jnp.int32, (16, 128), 1)

    def emit(comp, mode, real, imag):
        first = jnp.where(lane < 64, real, pltpu.roll(imag, 64, 1))
        second = jnp.where(lane < 64, pltpu.roll(real, 64, 1), imag)
        unit = 4 * comp + 2 * mode
        send1[16 * unit : 16 * unit + 16, :] = first.astype(BF16)
        send1[16 * unit + 16 : 16 * unit + 32, :] = second.astype(BF16)

    def add(total, term):
        return term if total is None else total + term

    level_lam = [moduli[0, phase] for phase in range(NPHASE)]
    level_mu = [moduli[1, phase] for phase in range(NPHASE)]
    shared = [[None, None] for _ in range(MODES)]
    sums = [[[None, None] for _ in range(MODES)] for _ in range(3)]
    for plane in range(XW):
        phases = labels[plane]
        shift_lam = contrast(phases, level_lam, lam0, 1.0)
        shift_mu = contrast(phases, level_mu, mu0, 2.0)
        shear[plane] = shift_mu
        parts = [strain[comp, plane].astype(F32) for comp in range(3)]
        trace = shift_lam * (parts[0] + parts[1] + parts[2])
        parts = [shift_mu * part for part in parts]
        for mode in range(MODES):
            for side, weight in enumerate(wave(mode, plane)):
                if weight == 0.0:
                    continue
                shared[mode][side] = add(shared[mode][side], weight * trace)
                for comp in range(3):
                    sums[comp][mode][side] = add(sums[comp][mode][side], weight * parts[comp])
    for comp in range(3):
        for mode in range(MODES):
            emit(comp, mode, sums[comp][mode][0] + shared[mode][0], sums[comp][mode][1] + shared[mode][1])
    sums = [[[None, None] for _ in range(MODES)] for _ in range(3)]
    for plane in range(XW):
        shift_mu = shear[plane]
        parts = [shift_mu * strain[3 + comp, plane].astype(F32) for comp in range(3)]
        for mode in range(MODES):
            for side, weight in enumerate(wave(mode, plane)):
                if weight == 0.0:
                    continue
                for comp in range(3):
                    sums[comp][mode][side] = add(sums[comp][mode][side], weight * parts[comp])
    for comp in range(3):
        for mode in range(MODES):
            emit(3 + comp, mode, sums[comp][mode][0], sums[comp][mode][1])

    greetings = jnp.where(works_y, UNITS_Y - 1, UNITS_Y) + jnp.where(works_z, UNITS_Z - 1, UNITS_Z)
    pl.semaphore_wait(barrier, greetings)

    def tile(index, rows=16):
        return pl.ds(pl.multiple_of(index * rows, rows), rows)

    base = place_unit(pencil - jnp.where(works_y, 0, 3))

    def send_first(step):
        unit = lax.rem(base + step, UNITS_Y)
        pltpu.make_async_remote_copy(
            src_ref=send1.at[tile(unit)],
            dst_ref=land1.at[tile(pencil)],
            send_sem=send_sems.at[0],
            recv_sem=land_sems.at[0],
            device_id=(unit_place(unit), slab),
            device_id_type=MESH,
        ).start()

    @pl.when(works_y)
    def _():
        pltpu.make_async_copy(send1.at[tile(base)], land1.at[tile(pencil)], land_sems.at[0]).start()

    @pl.when(jnp.logical_not(works_y))
    def _():
        send_first(0)

    for step in range(1, UNITS_Y):
        send_first(step)

    for load in table_loads[:2]:
        load.wait()
    sin_y, cos_y = freq_y[0], freq_y[1]
    sin_z, cos_z = (jnp.tile(freq_z[i], (4, 1)) for i in range(2))
    cos_yz, sin_cos, cos_sin = cos_y * cos_z, sin_y * cos_z, cos_y * sin_z

    def exchange_2(step, own):
        owner = lax.rem(pencil + step, PENCIL)
        unit = place_unit(pencil)
        mine = unit_place(unit // 2)
        source = send2.at[tile(owner)]
        target = land2.at[tile(2 * slab + unit % 2)]
        if own:
            pltpu.make_async_copy(source, target, land_sems.at[1]).start()
        else:
            pltpu.make_async_remote_copy(
                src_ref=source,
                dst_ref=target,
                send_sem=send_sems.at[1],
                recv_sem=land_sems.at[1],
                device_id=(owner, mine),
                device_id_type=MESH,
            ).start()

    stays = unit_place(place_unit(pencil) // 2) == slab

    @pl.when(works_y)
    def _():
        table_loads[2].wait()
        pltpu.make_async_copy(land1, land1, land_sems.at[0]).wait()
        band = jnp.dot(along_y[...], with_swapped(land1[...]), preferred_element_type=F32)
        send2[...] = (band * (1 / math.sqrt(NY))).astype(BF16)

        @pl.when(stays)
        def _():
            exchange_2(0, True)

        @pl.when(jnp.logical_not(stays))
        def _():
            exchange_2(0, False)

        for step in range(1, PENCIL):
            exchange_2(step, False)

    for load in table_loads[3:]:
        load.wait()

    @pl.when(jnp.logical_not(works_y))
    def _():
        table_loads[2].wait()

    @pl.when(works_z)
    def _():
        unit = place_unit(slab)
        pltpu.make_async_copy(land2, land2, land_sems.at[1]).wait()
        band = transform_z(land2[...], coarse[...], turn, fine)
        for owner in range(SLAB):
            for half in range(2):
                pair = [band[8 * owner : 8 * owner + 8, 128 * q : 128 * q + 128] for q in (2 * half, 2 * half + 1)]
                start = 32 * owner + 16 * half
                send3[start : start + 16, :] = jnp.concatenate(pair, 0).astype(BF16)
        pltpu.make_async_copy(send3.at[tile(slab, 32)], land3.at[tile(unit, 32)], land_sems.at[2]).start()
        for step in range(1, SLAB):
            owner = lax.rem(slab + step, SLAB)
            pltpu.make_async_remote_copy(
                src_ref=send3.at[tile(owner, 32)],
                dst_ref=land3.at[tile(unit, 32)],
                send_sem=send_sems.at[2],
                recv_sem=land_sems.at[2],
                device_id=(pencil, owner),
                device_id_type=MESH,
            ).start()

    factor = (lam0 + mu0) / (mu0 * (lam0 + 2.0 * mu0))
    half_mu = 1.0 / (2.0 * mu0)
    pltpu.make_async_copy(land3, land3, land_sems.at[2]).wait()
    for mode in range(MODES):
        angle = math.pi / NX * (KX0 + mode)
        sin_x, cos_x = math.sin(angle), math.cos(angle)
        qx, qy, qz = sin_x * cos_yz, cos_x * sin_cos, cos_x * cos_sin
        inverse = 1.0 / jnp.maximum(qx * qx + qy * qy + qz * qz, Q_FLOOR)
        first = half_mu * inverse
        second = factor * inverse * inverse
        spectrum = []
        for comp in range(COMPS):
            start = 32 * (2 * comp + mode)
            spectrum.append(land3[start : start + 32, :].astype(F32))
        txx, tyy, tzz, tyz, txz, txy = spectrum
        vecx = txx * qx + txy * qy + txz * qz
        vecy = txy * qx + tyy * qy + tyz * qz
        vecz = txz * qx + tyz * qy + tzz * qz
        inner = second * (qx * vecx + qy * vecy + qz * vecz)
        vecx, vecy, vecz = first * vecx, first * vecy, first * vecz
        results = (
            qx * (inner * qx - 2.0 * vecx),
            qy * (inner * qy - 2.0 * vecy),
            qz * (inner * qz - 2.0 * vecz),
            inner * qy * qz - (qy * vecz + qz * vecy),
            inner * qx * qz - (qx * vecz + qz * vecx),
            inner * qx * qy - (qx * vecy + qy * vecx),
        )
        for comp, result in enumerate(results):
            for part in range(2):
                pieces = [result[8 * q + 4 * part : 8 * q + 4 * part + 4] for q in range(4)]
                out[comp, part, mode] = jnp.concatenate(pieces, 0)

    @pl.when(works_y)
    def _():
        gone = send1.at[pl.ds(0, 16 * (UNITS_Y - 1))]
        pltpu.make_async_copy(gone, gone, send_sems.at[0]).wait()

        @pl.when(stays)
        def _():
            gone = send2.at[pl.ds(0, 16 * (PENCIL - 1))]
            pltpu.make_async_copy(gone, gone, send_sems.at[1]).wait()

        @pl.when(jnp.logical_not(stays))
        def _():
            pltpu.make_async_copy(send2, send2, send_sems.at[1]).wait()

    @pl.when(jnp.logical_not(works_y))
    def _():
        pltpu.make_async_copy(send1, send1, send_sems.at[0]).wait()

    @pl.when(works_z)
    def _():
        gone = send3.at[pl.ds(0, 32 * (SLAB - 1))]
        pltpu.make_async_copy(gone, gone, send_sems.at[2]).wait()


def per_device(strain, labels, moduli):
    consts = tables()
    anywhere = pl.BlockSpec(memory_space=pl.ANY)
    return pl.pallas_call(
        kernel,
        out_shape=jax.ShapeDtypeStruct((COMPS, 2, MODES, 16, 128), F32),
        in_specs=[pl.BlockSpec(memory_space=pltpu.SMEM)] + [anywhere] * 8,
        out_specs=pl.BlockSpec(memory_space=pltpu.VMEM),
        scratch_shapes=[
            pltpu.VMEM((COMPS, XW, 16, 128), BF16),
            pltpu.VMEM((XW, 16, 128), jnp.int32),
            pltpu.VMEM((NY, 2 * NY), BF16),
            pltpu.VMEM((512, 1024), BF16),
            pltpu.VMEM((2, 32, 128), F32),
            pltpu.VMEM((4, 128, 128), BF16),
            pltpu.VMEM((2, 32, 128), F32),
            pltpu.VMEM((2, 8, 128), F32),
            pltpu.VMEM((XW, 16, 128), F32),
            pltpu.VMEM((16 * UNITS_Y, 128), BF16),
            pltpu.VMEM((16 * PENCIL, 128), BF16),
            pltpu.VMEM((16 * PENCIL, 128), BF16),
            pltpu.VMEM((32 * SLAB, 128), BF16),
            pltpu.VMEM((32 * SLAB, 128), BF16),
            pltpu.VMEM((32 * UNITS_Z, 128), BF16),
            pltpu.SemaphoreType.DMA((2,)),
            pltpu.SemaphoreType.DMA((6,)),
            pltpu.SemaphoreType.DMA((3,)),
            pltpu.SemaphoreType.DMA((3,)),
        ],
        compiler_params=pltpu.CompilerParams(
            collective_id=0, has_side_effects=True, vmem_limit_bytes=32 * 1024 * 1024
        ),
    )(moduli, strain, labels, *(jnp.asarray(const) for const in consts))


def solution(mesh):
    return jax.shard_map(
        per_device,
        mesh=mesh,
        in_specs=(P(None, None, "pencil", "slab"), P(None, "pencil", "slab"), P()),
        out_specs=P(None, None, None, "pencil", "slab"),
        check_vma=False,
    )
```

time: 196 us -> 57.5 us (0.29); the launches traced: 193 us -> 57.1 us
  waiting for transfers between devices: 149 us -> 0 us
  Pallas kernels: 0 us -> 47.6 us
  between operations: 21.1 us -> 0.02 us
  other arithmetic: 9.92 us -> 0 us
  matrix products: 9 us -> 0 us
  local copies, waits for them, and re-layouts: 3.62 us -> 9.49 us
    all_gather x2 -> x0, waiting for transfers between devices: 149 us -> none  [the longest x1 74.9 us: per_device(): piece = lax.all_gather(x_band, 'pencil', axis=3, tiled=True)]
    pallas_call x0 -> x1, Pallas kernels: none -> 47.6 us  [per_device(): pl.pallas_call(kernel, out_shape=jax.ShapeDtypeStruct((COMPS, 2, MODES, 1...]
    unnamed x6 -> x19, local copies, waits for them, and re-layouts: 0.24 us -> 9.49 us
    dot_general x6 -> x0, matrix products: 9 us -> none  [the longest x1 3.06 us: along_last(): jnp.einsum('okrz,crmyz->comyk', low, data, preferred_element_type=jnp.flo...]
    mul x5 -> x0, other arithmetic: 4.74 us -> none  [the longest x2 4.45 us: twiddle(): sine = jnp.sin(angle) * scale]
    slice x2 -> x0, local copies, waits for them, and re-layouts: 2.69 us -> none  [the longest x1 1.66 us: polarize(): shift_lam = jnp.where(hit, moduli[0, phase] - lam0, shift_lam)]
    another operation x4 -> x0, other arithmetic: 1.96 us -> none  [the longest x2 1.85 us: twiddle(): jnp.stack([jnp.stack([cosine, sine], 1), jnp.stack([-sine, cosine], 1)], 0)]
  transfers between devices with their start and end apart: 2 -> 0, of which waited for: 2 -> 0; matrix products, arithmetic and copies ran while one was open for 3% -> 0% of each run, Pallas kernels for 0% -> 0%
where the time goes in v1:
time: 57.5 us; the launch traced here: 57.1 us
  Pallas kernels  47.6 us (83%)
  local copies, waits for them, and re-layouts  9.49 us (17%)
    pallas_call x1, Pallas kernels, per_device(): pl.pallas_call(kernel, out_shape=jax.ShapeDtypeStruct((COMPS, 2, MODES, 1...  47.6 us
    unnamed x19, local copies, waits for them, and re-layouts  9.49 us

profile of v1, /device:TPU:1, one launch (start us, length us, event | category | flops | bytes accessed | tf_op | source)
XLA Modules:
  0.0 57.1 jit_solution(5968802389725219233)
XLA Ops:
  0.0 0.0 copy-start
  0.0 1.2 %copy-done = f32[32,2,32,128]{3,2,1,0:T(8,128)S(1)} copy-done((f32[32,2,32,128]{3,2,1,0:T(8,128)S(1)}, f32[32,2,32,128]{3,2,1,0:T(8,128)}, u32[]{:S(2)}) %copy-start) | copy-done | bytes 1048600
  1.2 0.0 copy-start.1
  1.2 1.2 %copy-done.1 = bf16[512,1024]{1,0:T(8,128)(2,1)S(1)} copy-done((bf16[512,1024]{1,0:T(8,128)(2,1)S(1)}, bf16[512,1024]{1,0:T(8,128)(2,1)}, u32[]{:S(2)}) %copy-start.1) | copy-done | bytes 1048600
  2.5 0.0 copy-start.2
  2.5 1.2 %copy-done.2 = bf16[512,1024]{1,0:T(8,128)(2,1)S(1)} copy-done((bf16[512,1024]{1,0:T(8,128)(2,1)S(1)}, bf16[512,1024]{1,0:T(8,128)(2,1)}, u32[]{:S(2)}) %copy-start.2) | copy-done | bytes 1048600
  3.7 0.0 copy-start.3
  3.7 1.0 %copy-done.3 = bf16[6,16,16,128]{3,2,1,0:T(8,128)(2,1)S(1)} copy-done((bf16[6,16,16,128]{3,2,1,0:T(8,128)(2,1)S(1)}, bf16[6,16,16,128]{3,2,1,0:T(8,128)(2,1)}, u32[]{:S(2)}) %copy-start.3) | copy-done | bytes 393240
  4.7 0.0 copy-start.4
  4.7 0.9 %copy-done.4 = s32[16,16,128]{2,1,0:T(8,128)S(1)} copy-done((s32[16,16,128]{2,1,0:T(8,128)S(1)}, s32[16,16,128]{2,1,0:T(8,128)}, u32[]{:S(2)}) %copy-start.4) | copy-done | bytes 131096
  5.6 0.0 copy-start.5
  5.6 0.9 %copy-done.5 = f32[16,2,8,128]{3,2,1,0:T(8,128)S(1)} copy-done((f32[16,2,8,128]{3,2,1,0:T(8,128)S(1)}, f32[16,2,8,128]{3,2,1,0:T(8,128)}, u32[]{:S(2)}) %copy-start.5) | copy-done | bytes 131096
  6.5 0.0 copy-start.6
  6.5 0.9 %copy-done.6 = bf16[4,128,128]{2,1,0:T(8,128)(2,1)S(1)} copy-done((bf16[4,128,128]{2,1,0:T(8,128)(2,1)S(1)}, bf16[4,128,128]{2,1,0:T(8,128)(2,1)}, u32[]{:S(2)}) %copy-start.6) | copy-done | bytes 131096
  7.4 0.0 copy-start.7
  7.4 0.8 %copy-done.7 = f32[2,32,128]{2,1,0:T(8,128)S(1)} copy-done((f32[2,32,128]{2,1,0:T(8,128)S(1)}, f32[2,32,128]{2,1,0:T(8,128)}, u32[]{:S(2)}) %copy-start.7) | copy-done | bytes 32792
  8.1 0.0 copy-start.8
  8.1 0.7 %copy-done.8 = f32[2,4]{1,0:T(2,128)S(1)} copy-done((f32[2,4]{1,0:T(2,128)S(1)}, f32[2,4]{1,0:T(2,128)}, u32[]{:S(2)}) %copy-start.8) | copy-done | bytes 56
  8.8 47.6 %shard_map.91 = f32[6,2,2,16,128]{4,3,2,1,0:T(8,128)S(1)} custom-call(f32[2,4]{1,0:T(2,128)S(1)} %copy-done.8, bf16[6,16,16,128]{3,2,1,0:T(8,128)(2,1)S(1)} %copy-done.3, s32[16,16,128]{2,1,0:T(8,128)S(1)} %copy-done.4, bf16[512,1024]{1,0:T(8,128)(2,1)S(1)} %copy-done.2, bf16[512,1024]{1,0:T(8,128)(2,1)S(1)} %copy-done.1, f32[2,32,128]{2,1,0:T(8,128)S(1)} %copy-done.7, ...), custom_call_target="tpu_custom_call" | custom-call | tf_op jit(solution)/shard_map/pallas_call | solution.py:396
  56.5 0.7 %copy.11 = f32[6,2,2,16,128]{4,3,2,1,0:T(8,128)} copy(f32[6,2,2,16,128]{4,3,2,1,0:T(8,128)S(1)} %shard_map.91) | data formatting | bytes 393216
Async XLA Ops:
  0.0 1.2 %copy-start = (f32[32,2,32,128]{3,2,1,0:T(8,128)S(1)}, f32[32,2,32,128]{3,2,1,0:T(8,128)}, u32[]{:S(2)}) copy-start(f32[32,2,32,128]{3,2,1,0:T(8,128)} %constant.16.clone.freq_y_hbm) | copy-start | bytes 3145732
  1.2 1.2 %copy-start.1 = (bf16[512,1024]{1,0:T(8,128)(2,1)S(1)}, bf16[512,1024]{1,0:T(8,128)(2,1)}, u32[]{:S(2)}) copy-start(bf16[512,1024]{1,0:T(8,128)(2,1)} %constant.13.clone.coarse_hbm) | copy-start | bytes 3145732
  2.5 1.2 %copy-start.2 = (bf16[512,1024]{1,0:T(8,128)(2,1)S(1)}, bf16[512,1024]{1,0:T(8,128)(2,1)}, u32[]{:S(2)}) copy-start(bf16[512,1024]{1,0:T(8,128)(2,1)} %constant.12.clone.along_y_hbm) | copy-start | bytes 3145732
  3.7 1.0 %copy-start.3 = (bf16[6,16,16,128]{3,2,1,0:T(8,128)(2,1)S(1)}, bf16[6,16,16,128]{3,2,1,0:T(8,128)(2,1)}, u32[]{:S(2)}) copy-start(bf16[6,16,16,128]{3,2,1,0:T(8,128)(2,1)} %strain_hbm.1) | copy-start | bytes 1179652
  4.7 0.9 %copy-start.4 = (s32[16,16,128]{2,1,0:T(8,128)S(1)}, s32[16,16,128]{2,1,0:T(8,128)}, u32[]{:S(2)}) copy-start(s32[16,16,128]{2,1,0:T(8,128)} %labels_hbm.1) | copy-start | bytes 393220
  5.6 0.9 %copy-start.5 = (f32[16,2,8,128]{3,2,1,0:T(8,128)S(1)}, f32[16,2,8,128]{3,2,1,0:T(8,128)}, u32[]{:S(2)}) copy-start(f32[16,2,8,128]{3,2,1,0:T(8,128)} %constant.17.clone.freq_z_hbm) | copy-start | bytes 393220
  6.5 0.9 %copy-start.6 = (bf16[4,128,128]{2,1,0:T(8,128)(2,1)S(1)}, bf16[4,128,128]{2,1,0:T(8,128)(2,1)}, u32[]{:S(2)}) copy-start(bf16[4,128,128]{2,1,0:T(8,128)(2,1)} %constant.15.clone.fine_hbm) | copy-start | bytes 393220
  7.4 0.8 %copy-start.7 = (f32[2,32,128]{2,1,0:T(8,128)S(1)}, f32[2,32,128]{2,1,0:T(8,128)}, u32[]{:S(2)}) copy-start(f32[2,32,128]{2,1,0:T(8,128)} %constant.14.clone.turn_hbm) | copy-start | bytes 98308
  8.1 0.7 %copy-start.8 = (f32[2,4]{1,0:T(2,128)S(1)}, f32[2,4]{1,0:T(2,128)}, u32[]{:S(2)}) copy-start(f32[2,4]{1,0:T(2,128)} %moduli.1) | copy-start | bytes 100

commit v2 on v1

--- a/solution.py
+++ b/solution.py
@@ -17,12 +17,17 @@
 F32, BF16 = jnp.float32, jnp.bfloat16
 
 
-def unit_place(unit):
-    return unit // 3 * 4 + unit % 3
-
-
-def place_unit(place):
-    return place // 4 * 3 + place % 4
+def z_place(unit, owner):
+    return lax.rem(unit + owner, UNITS_Z)
+
+
+def z_unit(place, owner):
+    return lax.rem(place + 3 * UNITS_Z - owner, UNITS_Z)
+
+
+def far_first(chips, each):
+    order = sorted(range(chips), key=lambda step: -min(step, chips - step))
+    return [chip * each + i for chip in order for i in reversed(range(each))]
 
 
 def tables():
@@ -98,7 +103,7 @@
 
 
 def kernel(
-    moduli,
+    moduli_hbm,
     strain_hbm,
     labels_hbm,
     along_y_hbm,
@@ -108,6 +113,7 @@
     freq_y_hbm,
     freq_z_hbm,
     out,
+    moduli,
     strain,
     labels,
     along_y,
@@ -130,9 +136,11 @@
 ):
     pencil = lax.axis_index("pencil")
     slab = lax.axis_index("slab")
-    works_y = pencil % 4 < 3
-    works_z = slab % 4 < 3
-
+    works_y = pencil < UNITS_Y
+    works_z = slab < UNITS_Z
+
+    moduli_load = pltpu.make_async_copy(moduli_hbm, moduli, in_sems.at[2])
+    moduli_load.start()
     loads = [
         pltpu.make_async_copy(strain_hbm, strain, in_sems.at[0]),
         pltpu.make_async_copy(labels_hbm, labels, in_sems.at[1]),
@@ -155,22 +163,17 @@
 
     @pl.when(works_y)
     def _():
-        def greet(step, carry):
+        for step in far_first(8, 4)[:-1]:
             other = lax.rem(pencil + step, PENCIL)
             pl.semaphore_signal(barrier, inc=1, device_id=(other, slab), device_id_type=MESH)
-            return carry
-
-        lax.fori_loop(1, PENCIL, greet, 0)
 
     @pl.when(works_z)
     def _():
-        def greet(step, carry):
+        for step in far_first(8, 2)[:-1]:
             other = lax.rem(slab + step, SLAB)
             pl.semaphore_signal(barrier, inc=1, device_id=(pencil, other), device_id_type=MESH)
-            return carry
-
-        lax.fori_loop(1, SLAB, greet, 0)
-
+
+    moduli_load.wait()
     lam0 = 0.5 * (
         jnp.minimum(jnp.minimum(moduli[0, 0], moduli[0, 1]), jnp.minimum(moduli[0, 2], moduli[0, 3]))
         + jnp.maximum(jnp.maximum(moduli[0, 0], moduli[0, 1]), jnp.maximum(moduli[0, 2], moduli[0, 3]))
@@ -236,29 +239,26 @@
     def tile(index, rows=16):
         return pl.ds(pl.multiple_of(index * rows, rows), rows)
 
-    base = place_unit(pencil - jnp.where(works_y, 0, 3))
-
-    def send_first(step):
-        unit = lax.rem(base + step, UNITS_Y)
+    def send_first(unit):
         pltpu.make_async_remote_copy(
             src_ref=send1.at[tile(unit)],
             dst_ref=land1.at[tile(pencil)],
             send_sem=send_sems.at[0],
             recv_sem=land_sems.at[0],
-            device_id=(unit_place(unit), slab),
+            device_id=(unit, slab),
             device_id_type=MESH,
         ).start()
 
+    for step in far_first(8, 4)[:-1]:
+        unit = lax.rem(pencil + step, PENCIL)
+
+        @pl.when(unit < UNITS_Y)
+        def _():
+            send_first(unit)
+
     @pl.when(works_y)
     def _():
-        pltpu.make_async_copy(send1.at[tile(base)], land1.at[tile(pencil)], land_sems.at[0]).start()
-
-    @pl.when(jnp.logical_not(works_y))
-    def _():
-        send_first(0)
-
-    for step in range(1, UNITS_Y):
-        send_first(step)
+        pltpu.make_async_copy(send1.at[tile(pencil)], land1.at[tile(pencil)], land_sems.at[0]).start()
 
     for load in table_loads[:2]:
         load.wait()
@@ -268,10 +268,9 @@
 
     def exchange_2(step, own):
         owner = lax.rem(pencil + step, PENCIL)
-        unit = place_unit(pencil)
-        mine = unit_place(unit // 2)
+        mine = z_place(pencil // 2, owner)
         source = send2.at[tile(owner)]
-        target = land2.at[tile(2 * slab + unit % 2)]
+        target = land2.at[tile(2 * slab + pencil % 2)]
         if own:
             pltpu.make_async_copy(source, target, land_sems.at[1]).start()
         else:
@@ -284,7 +283,7 @@
                 device_id_type=MESH,
             ).start()
 
-    stays = unit_place(place_unit(pencil) // 2) == slab
+    stays = z_place(pencil // 2, pencil) == slab
 
     @pl.when(works_y)
     def _():
@@ -293,6 +292,9 @@
         band = jnp.dot(along_y[...], with_swapped(land1[...]), preferred_element_type=F32)
         send2[...] = (band * (1 / math.sqrt(NY))).astype(BF16)
 
+        for step in far_first(8, 4)[:-1]:
+            exchange_2(step, False)
+
         @pl.when(stays)
         def _():
             exchange_2(0, True)
@@ -301,9 +303,6 @@
         def _():
             exchange_2(0, False)
 
-        for step in range(1, PENCIL):
-            exchange_2(step, False)
-
     for load in table_loads[3:]:
         load.wait()
 
@@ -313,7 +312,7 @@
 
     @pl.when(works_z)
     def _():
-        unit = place_unit(slab)
+        unit = z_unit(slab, pencil)
         pltpu.make_async_copy(land2, land2, land_sems.at[1]).wait()
         band = transform_z(land2[...], coarse[...], turn, fine)
         for owner in range(SLAB):
@@ -321,8 +320,7 @@
                 pair = [band[8 * owner : 8 * owner + 8, 128 * q : 128 * q + 128] for q in (2 * half, 2 * half + 1)]
                 start = 32 * owner + 16 * half
                 send3[start : start + 16, :] = jnp.concatenate(pair, 0).astype(BF16)
-        pltpu.make_async_copy(send3.at[tile(slab, 32)], land3.at[tile(unit, 32)], land_sems.at[2]).start()
-        for step in range(1, SLAB):
+        for step in far_first(8, 2)[:-1]:
             owner = lax.rem(slab + step, SLAB)
             pltpu.make_async_remote_copy(
                 src_ref=send3.at[tile(owner, 32)],
@@ -332,6 +330,7 @@
                 device_id=(pencil, owner),
                 device_id_type=MESH,
             ).start()
+        pltpu.make_async_copy(send3.at[tile(slab, 32)], land3.at[tile(unit, 32)], land_sems.at[2]).start()
 
     factor = (lam0 + mu0) / (mu0 * (lam0 + 2.0 * mu0))
     half_mu = 1.0 / (2.0 * mu0)
@@ -391,14 +390,18 @@
 
 
 def per_device(strain, labels, moduli):
-    consts = tables()
-    anywhere = pl.BlockSpec(memory_space=pl.ANY)
+    consts = [jnp.asarray(const) for const in tables()]
+    moduli, strain, labels, *consts = [
+        pltpu.with_memory_space_constraint(x, pltpu.HBM) for x in (moduli, strain, labels, *consts)
+    ]
+    anywhere = pl.BlockSpec(memory_space=pltpu.HBM)
     return pl.pallas_call(
         kernel,
         out_shape=jax.ShapeDtypeStruct((COMPS, 2, MODES, 16, 128), F32),
-        in_specs=[pl.BlockSpec(memory_space=pltpu.SMEM)] + [anywhere] * 8,
+        in_specs=[anywhere] * 9,
         out_specs=pl.BlockSpec(memory_space=pltpu.VMEM),
         scratch_shapes=[
+            pltpu.SMEM((2, NPHASE), F32),
             pltpu.VMEM((COMPS, XW, 16, 128), BF16),
             pltpu.VMEM((XW, 16, 128), jnp.int32),
             pltpu.VMEM((NY, 2 * NY), BF16),
@@ -414,7 +417,7 @@
             pltpu.VMEM((32 * SLAB, 128), BF16),
             pltpu.VMEM((32 * SLAB, 128), BF16),
             pltpu.VMEM((32 * UNITS_Z, 128), BF16),
-            pltpu.SemaphoreType.DMA((2,)),
+            pltpu.SemaphoreType.DMA((3,)),
             pltpu.SemaphoreType.DMA((6,)),
             pltpu.SemaphoreType.DMA((3,)),
             pltpu.SemaphoreType.DMA((3,)),
@@ -422,7 +425,7 @@
         compiler_params=pltpu.CompilerParams(
             collective_id=0, has_side_effects=True, vmem_limit_bytes=32 * 1024 * 1024
         ),
-    )(moduli, strain, labels, *(jnp.asarray(const) for const in consts))
+    )(moduli, strain, labels, *consts)
 
 
 def solution(mesh):

time: 57.5 us -> 38.1 us (0.66)
  Pallas kernels: 47.6 us -> 37.2 us
  local copies, waits for them, and re-layouts: 9.49 us -> 0.68 us
    pallas_call x1, Pallas kernels: 47.6 us -> 37.2 us  [per_device(): pl.pallas_call(kernel, out_shape=jax.ShapeDtypeStruct((COMPS, 2, MODES, 1...]
    unnamed x19 -> x1, local copies, waits for them, and re-layouts: 9.49 us -> 0.68 us
where the time goes in v2:
time: 38.1 us; the launch traced here: 37.9 us
  Pallas kernels  37.2 us (98%)
  local copies, waits for them, and re-layouts  0.68 us (2%)
    pallas_call x1, Pallas kernels, per_device(): pl.pallas_call(kernel, out_shape=jax.ShapeDtypeStruct((COMPS, 2, MODES, 1...  37.2 us

profile of v2, /device:TPU:1, one launch (start us, length us, event | category | flops | bytes accessed | tf_op | source)
XLA Modules:
  0.0 37.9 jit_solution(11175603693703856812)
XLA Ops:
  0.0 37.2 %shard_map.91 = f32[6,2,2,16,128]{4,3,2,1,0:T(8,128)S(1)} custom-call(f32[2,4]{1,0:T(2,128)} %moduli_hbm.1, bf16[6,16,16,128]{3,2,1,0:T(8,128)(2,1)} %strain_hbm.1, s32[16,16,128]{2,1,0:T(8,128)} %labels_hbm.1, bf16[512,1024]{1,0:T(8,128)(2,1)} %constant.12.clone.along_y_hbm, bf16[512,1024]{1,0:T(8,128)(2,1)} %constant.13.clone.coarse_hbm, ...), custom_call_target="tpu_custom_call" | custom-call | tf_op jit(solution)/shard_map/pallas_call | solution.py:398
  37.2 0.7 %copy.11 = f32[6,2,2,16,128]{4,3,2,1,0:T(8,128)} copy(f32[6,2,2,16,128]{4,3,2,1,0:T(8,128)S(1)} %shard_map.91) | data formatting | bytes 393216

commit v3 on v2

v3 whole, which is shorter than its diff:
```python
import math

import jax
import jax.numpy as jnp
import numpy as np
from jax import lax
from jax.experimental import pallas as pl
from jax.experimental.pallas import tpu as pltpu
from jax.sharding import PartitionSpec as P

MESH = pl.DeviceIdType.MESH
NX, NY, NZ = 2048, 512, 2048
XW, MODES, KX0, NPHASE, COMPS = 16, 2, 64, 4, 6
PENCIL, SLAB = 32, 16
UNITS = 12
SLAB_ORDER = (0, 1, 2, 3, 14, 15, 4, 5, 12, 13, 6, 7, 10, 11, 8, 9)
Q_FLOOR = 0.01
F32, BF16 = jnp.float32, jnp.bfloat16


def z_place(unit, owner):
    return lax.rem(lax.rem(unit + owner, UNITS) + SLAB - 4, SLAB)


def z_unit(place, owner):
    return lax.rem(lax.rem(place + 4, SLAB) + 3 * UNITS - owner, UNITS)


def far_first(chips, each):
    order = sorted(range(chips), key=lambda step: -min(step, chips - step))
    return [chip * each + i for chip in order for i in reversed(range(each))]


def parts_table(angle):
    cosine, sine = np.cos(angle), np.sin(angle)
    return np.stack([np.stack([cosine, sine], 1), np.stack([-sine, cosine], 1)])


def tables():
    angle = 2 * math.pi / NY * (np.outer(np.arange(NY), np.arange(NY)) % NY)
    along_y = parts_table(angle).reshape(2, PENCIL, 16, 2, PENCIL, 16)
    along_y = along_y.transpose(1, 0, 2, 4, 3, 5).reshape(2 * NY, 2 * NY)
    angle = 2 * math.pi / 16 * (np.outer(np.arange(16), np.arange(16)) % 16)
    coarse = np.einsum("obrs,kj->okbsrj", parts_table(angle), np.eye(16)).reshape(512, 512)
    angle = 2 * math.pi / NZ * np.outer(np.arange(16), np.arange(128))
    turn = np.stack([np.cos(angle), np.sin(angle)]) / math.sqrt(NZ)
    angle = 2 * math.pi / 128 * (np.outer(np.arange(128), np.arange(128)) % 128)
    fine = parts_table(angle).reshape(2, SLAB, 8, 256)[:, list(SLAB_ORDER)].transpose(1, 0, 2, 3)
    fine = np.stack([np.roll(fine, -delta, 2).reshape(256, 256) for delta in range(8)])
    angle = math.pi / NY * np.arange(NY).reshape(PENCIL, 16, 1)
    angle = np.broadcast_to(angle, (PENCIL, 16, 128))
    freq_y = np.stack([np.sin(angle), np.cos(angle)], 1)
    angle = math.pi / NZ * np.arange(NZ).reshape(SLAB, 1, 128)
    angle = np.broadcast_to(angle, (SLAB, 8, 128))
    freq_z = np.stack([np.sin(angle), np.cos(angle)], 1)
    return (
        along_y.astype(BF16),
        coarse.astype(BF16),
        turn.astype(np.float32),
        fine.astype(BF16),
        freq_y.astype(np.float32),
        freq_z.astype(np.float32),
    )


def transform_z(data, coarse, turn):
    mixed = jnp.dot(coarse, data, preferred_element_type=F32).reshape(2, 16, 16, 128)
    cosine, sine = turn[0][None], turn[1][None]
    real = mixed[0] * cosine + mixed[1] * sine
    imag = mixed[1] * cosine - mixed[0] * sine
    parts = [part.reshape(256, 128).astype(BF16) for part in (real, imag)]
    return jnp.concatenate(parts, 1)


def last_points(turned, fine, start, size):
    row = lax.broadcasted_iota(jnp.int32, (size, 256), 0)
    lane = lax.broadcasted_iota(jnp.int32, (size, 256), 1)
    shift = (lane // 16 - row) & 7
    result = None
    for delta in range(8):
        part = lax.dot_general(
            fine[delta, start : start + size, :], turned[delta], (((1,), (1,)), ((), ())), preferred_element_type=F32
        )
        result = part if result is None else jnp.where(shift == delta, part, result)
    return result


def contrast(labels, values, base, factor):
    levels = [(values[phase] - base) * factor for phase in range(NPHASE)]
    chosen = jnp.where(labels == 2, levels[2], levels[3])
    chosen = jnp.where(labels == 1, levels[1], chosen)
    return jnp.where(labels == 0, levels[0], chosen)


def wave(mode, plane):
    angle = 2 * math.pi / NX * ((KX0 + mode) * plane % NX)
    scale = 1 / math.sqrt(XW)
    return float(math.cos(angle) * scale), float(-math.sin(angle) * scale)


def kernel(
    moduli_hbm,
    strain_hbm,
    labels_hbm,
    along_y_hbm,
    coarse_hbm,
    turn_hbm,
    fine_hbm,
    freq_y_hbm,
    freq_z_hbm,
    out,
    moduli,
    strain,
    labels,
    along_y,
    coarse,
    turn,
    fine,
    freq_y,
    freq_z,
    shear,
    send1,
    land1,
    send2,
    land2,
    send3,
    land3,
    in_sems,
    table_sems,
    send_sems,
    land_sems,
):
    pencil = lax.axis_index("pencil")
    slab = lax.axis_index("slab")
    works_y = (pencil < 24) & (pencil % 2 == 0)
    unit_y = pencil // 4 * 2 + pencil % 4 // 2
    works_z = lax.rem(slab + 4, SLAB) < UNITS

    barrier = pltpu.get_barrier_semaphore()

    @pl.when(works_y)
    def _():
        for step in far_first(8, 4)[:-1]:
            other = lax.rem(pencil + step, PENCIL)
            pl.semaphore_signal(barrier, inc=1, device_id=(other, slab), device_id_type=MESH)

    @pl.when(works_z)
    def _():
        for step in far_first(8, 2)[:-1]:
            other = lax.rem(slab + step, SLAB)
            pl.semaphore_signal(barrier, inc=1, device_id=(pencil, other), device_id_type=MESH)

    moduli_load = pltpu.make_async_copy(moduli_hbm, moduli, in_sems.at[2])
    moduli_load.start()
    loads = [
        pltpu.make_async_copy(strain_hbm, strain, in_sems.at[0]),
        pltpu.make_async_copy(labels_hbm, labels, in_sems.at[1]),
    ]
    for load in loads:
        load.start()
    pairs = [
        (freq_y_hbm.at[pencil], freq_y),
        (freq_z_hbm.at[slab], freq_z),
        (along_y_hbm, along_y),
        (coarse_hbm, coarse),
        (turn_hbm, turn),
        (fine_hbm, fine),
    ]
    table_loads = [pltpu.make_async_copy(a, b, table_sems.at[i]) for i, (a, b) in enumerate(pairs)]
    for load in table_loads:
        load.start()

    moduli_load.wait()
    lam0 = 0.5 * (
        jnp.minimum(jnp.minimum(moduli[0, 0], moduli[0, 1]), jnp.minimum(moduli[0, 2], moduli[0, 3]))
        + jnp.maximum(jnp.maximum(moduli[0, 0], moduli[0, 1]), jnp.maximum(moduli[0, 2], moduli[0, 3]))
    )
    mu0 = 0.5 * (
        jnp.minimum(jnp.minimum(moduli[1, 0], moduli[1, 1]), jnp.minimum(moduli[1, 2], moduli[1, 3]))
        + jnp.maximum(jnp.maximum(moduli[1, 0], moduli[1, 1]), jnp.maximum(moduli[1, 2], moduli[1, 3]))
    )

    for load in loads:
        load.wait()

    def emit(comp, mode, real, imag):
        start = 32 * (2 * comp + mode)
        send1[start : start + 16, :] = real.astype(BF16)
        send1[start + 16 : start + 32, :] = imag.astype(BF16)

    def add(total, term):
        return term if total is None else total + term

    level_lam = [moduli[0, phase] for phase in range(NPHASE)]
    level_mu = [moduli[1, phase] for phase in range(NPHASE)]
    shared = [[None, None] for _ in range(MODES)]
    sums = [[[None, None] for _ in range(MODES)] for _ in range(3)]
    for plane in range(XW):
        phases = labels[plane]
        shift_lam = contrast(phases, level_lam, lam0, 1.0)
        shift_mu = contrast(phases, level_mu, mu0, 2.0)
        shear[plane] = shift_mu
        parts = [strain[comp, plane].astype(F32) for comp in range(3)]
        trace = shift_lam * (parts[0] + parts[1] + parts[2])
        parts = [shift_mu * part for part in parts]
        for mode in range(MODES):
            for side, weight in enumerate(wave(mode, plane)):
                if weight == 0.0:
                    continue
                shared[mode][side] = add(shared[mode][side], weight * trace)
                for comp in range(3):
                    sums[comp][mode][side] = add(sums[comp][mode][side], weight * parts[comp])
    for comp in range(3):
        for mode in range(MODES):
            emit(comp, mode, sums[comp][mode][0] + shared[mode][0], sums[comp][mode][1] + shared[mode][1])
    sums = [[[None, None] for _ in range(MODES)] for _ in range(3)]
    for plane in range(XW):
        shift_mu = shear[plane]
        parts = [shift_mu * strain[3 + comp, plane].astype(F32) for comp in range(3)]
        for mode in range(MODES):
            for side, weight in enumerate(wave(mode, plane)):
                if weight == 0.0:
                    continue
                for comp in range(3):
                    sums[comp][mode][side] = add(sums[comp][mode][side], weight * parts[comp])
    for comp in range(3):
        for mode in range(MODES):
            emit(3 + comp, mode, sums[comp][mode][0], sums[comp][mode][1])

    greetings = jnp.where(works_y, UNITS - 1, UNITS) + jnp.where(works_z, UNITS - 1, UNITS)
    pl.semaphore_wait(barrier, greetings)

    def tile(index):
        return pl.ds(pl.multiple_of(index * 32, 32), 32)

    for unit in (10, 11, 8, 9, 6, 7, 4, 5, 2, 3, 0, 1):
        place = 4 * (unit // 2) + 2 * (unit % 2)

        @pl.when(pencil != place)
        def _():
            pltpu.make_async_remote_copy(
                src_ref=send1.at[tile(unit)],
                dst_ref=land1.at[tile(pencil)],
                send_sem=send_sems.at[0],
                recv_sem=land_sems.at[0],
                device_id=(place, slab),
                device_id_type=MESH,
            ).start()

    @pl.when(works_y)
    def _():
        pltpu.make_async_copy(send1.at[tile(unit_y)], land1.at[tile(pencil)], land_sems.at[0]).start()

    for load in table_loads[:2]:
        load.wait()
    sin_y, cos_y = freq_y[0], freq_y[1]
    sin_z, cos_z = (jnp.tile(freq_z[i], (2, 1)) for i in range(2))
    cos_yz, sin_cos, cos_sin = cos_y * cos_z, sin_y * cos_z, cos_y * sin_z

    def exchange_2(owner, own):
        mine = z_place(unit_y, owner)
        source = send2.at[tile(owner)]
        target = land2.at[tile(slab)]
        if own:
            pltpu.make_async_copy(source, target, land_sems.at[1]).start()
        else:
            pltpu.make_async_remote_copy(
                src_ref=source,
                dst_ref=target,
                send_sem=send_sems.at[1],
                recv_sem=land_sems.at[1],
                device_id=(owner, mine),
                device_id_type=MESH,
            ).start()

    stays = z_place(unit_y, pencil) == slab

    @pl.when(works_y)
    def _():
        table_loads[2].wait()
        pltpu.make_async_copy(land1, land1, land_sems.at[0]).wait()
        for chunk in range(4):
            rows = slice(256 * chunk, 256 * chunk + 256)
            band = jnp.dot(along_y[rows, :], land1[...], preferred_element_type=F32)
            send2[rows, :] = (band * (1 / math.sqrt(NY))).astype(BF16)
            for owner in range(8 * chunk, 8 * chunk + 8):
                own = stays & (pencil == owner)

                @pl.when(own)
                def _():
                    exchange_2(owner, True)

                @pl.when(jnp.logical_not(own))
                def _():
                    exchange_2(owner, False)

    for load in table_loads[3:]:
        load.wait()

    @pl.when(jnp.logical_not(works_y))
    def _():
        table_loads[2].wait()

    @pl.when(works_z)
    def _():
        unit = z_unit(slab, pencil)
        pltpu.make_async_copy(land2, land2, land_sems.at[1]).wait()
        band = transform_z(land2[...], coarse[...], turn)
        blocks = [band[16 * k : 16 * k + 16] for k in range(16)]
        turned = [
            jnp.concatenate([blocks[8 * (k // 8) + (k - delta) % 8] for k in range(16)], 0) for delta in range(8)
        ]
        for chunk in range(2):
            points = last_points(turned, fine, 128 * chunk, 128)
            for place, owner in enumerate(SLAB_ORDER[8 * chunk : 8 * chunk + 8]):
                for part in range(2):
                    row, start = 16 * place + 8 * part, 32 * owner + 16 * part
                    halves = [points[row : row + 8, 128 * half : 128 * half + 128] for half in range(2)]
                    send3[start : start + 16, :] = jnp.concatenate(halves, 0).astype(BF16)
            for owner in SLAB_ORDER[8 * chunk : 8 * chunk + 8]:
                source, target = send3.at[tile(owner)], land3.at[tile(unit)]

                @pl.when(slab == owner)
                def _():
                    pltpu.make_async_copy(source, target, land_sems.at[2]).start()

                @pl.when(slab != owner)
                def _():
                    pltpu.make_async_remote_copy(
                        src_ref=source,
                        dst_ref=target,
                        send_sem=send_sems.at[2],
                        recv_sem=land_sems.at[2],
                        device_id=(pencil, owner),
                        device_id_type=MESH,
                    ).start()

    factor = (lam0 + mu0) / (mu0 * (lam0 + 2.0 * mu0))
    half_mu = 1.0 / (2.0 * mu0)
    weights = []
    for mode in range(MODES):
        angle = math.pi / NX * (KX0 + mode)
        sin_x, cos_x = math.sin(angle), math.cos(angle)
        qx, qy, qz = sin_x * cos_yz, cos_x * sin_cos, cos_x * cos_sin
        inverse = 1.0 / jnp.maximum(qx * qx + qy * qy + qz * qz, Q_FLOOR)
        weights.append((qx, qy, qz, half_mu * inverse, factor * inverse * inverse))
    pltpu.make_async_copy(land3, land3, land_sems.at[2]).wait()
    for mode in range(MODES):
        qx, qy, qz, first, second = weights[mode]
        for part in range(2):
            spectrum = []
            for comp in range(COMPS):
                start = 32 * (2 * comp + mode) + 16 * part
                spectrum.append(land3[start : start + 16, :].astype(F32))
            txx, tyy, tzz, tyz, txz, txy = spectrum
            vecx = txx * qx + txy * qy + txz * qz
            vecy = txy * qx + tyy * qy + tyz * qz
            vecz = txz * qx + tyz * qy + tzz * qz
            inner = second * (qx * vecx + qy * vecy + qz * vecz)
            vecx, vecy, vecz = first * vecx, first * vecy, first * vecz
            out[0, part, mode] = qx * (inner * qx - 2.0 * vecx)
            out[1, part, mode] = qy * (inner * qy - 2.0 * vecy)
            out[2, part, mode] = qz * (inner * qz - 2.0 * vecz)
            out[3, part, mode] = inner * qy * qz - (qy * vecz + qz * vecy)
            out[4, part, mode] = inner * qx * qz - (qx * vecz + qz * vecx)
            out[5, part, mode] = inner * qx * qy - (qx * vecy + qy * vecx)

    @pl.when(works_y)
    def _():
        gone = send1.at[pl.ds(0, 32 * (UNITS - 1))]
        pltpu.make_async_copy(gone, gone, send_sems.at[0]).wait()

        @pl.when(stays)
        def _():
            gone = send2.at[pl.ds(0, 32 * (PENCIL - 1))]
            pltpu.make_async_copy(gone, gone, send_sems.at[1]).wait()

        @pl.when(jnp.logical_not(stays))
        def _():
            pltpu.make_async_copy(send2, send2, send_sems.at[1]).wait()

    @pl.when(jnp.logical_not(works_y))
    def _():
        pltpu.make_async_copy(send1, send1, send_sems.at[0]).wait()

    @pl.when(works_z)
    def _():
        gone = send3.at[pl.ds(0, 32 * (SLAB - 1))]
        pltpu.make_async_copy(gone, gone, send_sems.at[2]).wait()


def per_device(strain, labels, moduli):
    consts = [jnp.asarray(const) for const in tables()]
    moduli, strain, labels, *consts = [
        pltpu.with_memory_space_constraint(x, pltpu.HBM) for x in (moduli, strain, labels, *consts)
    ]
    anywhere = pl.BlockSpec(memory_space=pltpu.HBM)
    return pl.pallas_call(
        kernel,
        out_shape=jax.ShapeDtypeStruct((COMPS, 2, MODES, 16, 128), F32),
        in_specs=[anywhere] * 9,
        out_specs=pl.BlockSpec(memory_space=pltpu.VMEM),
        scratch_shapes=[
            pltpu.SMEM((2, NPHASE), F32),
            pltpu.VMEM((COMPS, XW, 16, 128), BF16),
            pltpu.VMEM((XW, 16, 128), jnp.int32),
            pltpu.VMEM((2 * NY, 2 * NY), BF16),
            pltpu.VMEM((512, 512), BF16),
            pltpu.VMEM((2, 16, 128), F32),
            pltpu.VMEM((8, 256, 256), BF16),
            pltpu.VMEM((2, 16, 128), F32),
            pltpu.VMEM((2, 8, 128), F32),
            pltpu.VMEM((XW, 16, 128), F32),
            pltpu.VMEM((32 * UNITS, 128), BF16),
            pltpu.VMEM((32 * PENCIL, 128), BF16),
            pltpu.VMEM((32 * PENCIL, 128), BF16),
            pltpu.VMEM((32 * SLAB, 128), BF16),
            pltpu.VMEM((32 * SLAB, 128), BF16),
            pltpu.VMEM((32 * UNITS, 128), BF16),
            pltpu.SemaphoreType.DMA((3,)),
            pltpu.SemaphoreType.DMA((6,)),
            pltpu.SemaphoreType.DMA((3,)),
            pltpu.SemaphoreType.DMA((3,)),
        ],
        compiler_params=pltpu.CompilerParams(
            collective_id=0, has_side_effects=True, vmem_limit_bytes=32 * 1024 * 1024
        ),
    )(moduli, strain, labels, *consts)


def solution(mesh):
    return jax.shard_map(
        per_device,
        mesh=mesh,
        in_specs=(P(None, None, "pencil", "slab"), P(None, "pencil", "slab"), P()),
        out_specs=P(None, None, None, "pencil", "slab"),
        check_vma=False,
    )
```

time: 38.1 us -> 35.5 us (0.932)
  Pallas kernels: 37.2 us -> 34.5 us
    pallas_call x1, Pallas kernels: 37.2 us -> 34.5 us  [per_device(): pl.pallas_call(kernel, out_shape=jax.ShapeDtypeStruct((COMPS, 2, MODES, 1...]
where the time goes in v3:
time: 35.5 us; the launch traced here: 35.2 us
  Pallas kernels  34.5 us (97%)
  local copies, waits for them, and re-layouts  0.68 us (2%)
    pallas_call x1, Pallas kernels, per_device(): pl.pallas_call(kernel, out_shape=jax.ShapeDtypeStruct((COMPS, 2, MODES, 1...  34.5 us

profile of v3, /device:TPU:1, one launch (start us, length us, event | category | flops | bytes accessed | tf_op | source)
XLA Modules:
  0.0 35.2 jit_solution(18028503677647988151)
XLA Ops:
  0.0 34.5 %shard_map.91 = f32[6,2,2,16,128]{4,3,2,1,0:T(8,128)S(1)} custom-call(f32[2,4]{1,0:T(2,128)} %moduli_hbm.1, bf16[6,16,16,128]{3,2,1,0:T(8,128)(2,1)} %strain_hbm.1, s32[16,16,128]{2,1,0:T(8,128)} %labels_hbm.1, bf16[1024,1024]{1,0:T(8,128)(2,1)} %constant.12.clone.along_y_hbm, bf16[512,512]{1,0:T(8,128)(2,1)} %constant.13.clone.coarse_hbm, ...), custom_call_target="tpu_custom_call" | custom-call | tf_op jit(solution)/shard_map/pallas_call | solution.py:398
  34.5 0.7 %copy.11 = f32[6,2,2,16,128]{4,3,2,1,0:T(8,128)} copy(f32[6,2,2,16,128]{4,3,2,1,0:T(8,128)S(1)} %shard_map.91) | data formatting | bytes 393216

commit v4 on v3

--- a/solution.py
+++ b/solution.py
@@ -18,12 +18,16 @@
 F32, BF16 = jnp.float32, jnp.bfloat16
 
 
+def wrap(index, size):
+    return jnp.where(index >= size, index - size, index)
+
+
 def z_place(unit, owner):
-    return lax.rem(lax.rem(unit + owner, UNITS) + SLAB - 4, SLAB)
+    return wrap(wrap(unit + 5 * owner % UNITS, UNITS) + SLAB - 4, SLAB)
 
 
 def z_unit(place, owner):
-    return lax.rem(lax.rem(place + 4, SLAB) + 3 * UNITS - owner, UNITS)
+    return lax.rem(wrap(place + 4, SLAB) + 13 * UNITS - 5 * owner, UNITS)
 
 
 def far_first(chips, each):
@@ -46,7 +50,7 @@
     turn = np.stack([np.cos(angle), np.sin(angle)]) / math.sqrt(NZ)
     angle = 2 * math.pi / 128 * (np.outer(np.arange(128), np.arange(128)) % 128)
     fine = parts_table(angle).reshape(2, SLAB, 8, 256)[:, list(SLAB_ORDER)].transpose(1, 0, 2, 3)
-    fine = np.stack([np.roll(fine, -delta, 2).reshape(256, 256) for delta in range(8)])
+    fine = fine.reshape(256, 256)
     angle = math.pi / NY * np.arange(NY).reshape(PENCIL, 16, 1)
     angle = np.broadcast_to(angle, (PENCIL, 16, 128))
     freq_y = np.stack([np.sin(angle), np.cos(angle)], 1)
@@ -72,17 +76,26 @@
     return jnp.concatenate(parts, 1)
 
 
-def last_points(turned, fine, start, size):
-    row = lax.broadcasted_iota(jnp.int32, (size, 256), 0)
-    lane = lax.broadcasted_iota(jnp.int32, (size, 256), 1)
-    shift = (lane // 16 - row) & 7
-    result = None
-    for delta in range(8):
-        part = lax.dot_general(
-            fine[delta, start : start + size, :], turned[delta], (((1,), (1,)), ((), ())), preferred_element_type=F32
-        )
-        result = part if result is None else jnp.where(shift == delta, part, result)
-    return result
+def exchange_bit(values, axis, bit):
+    size = values.shape[axis]
+    if 2 * bit == size:
+        return pltpu.roll(values, bit, axis)
+    index = lax.broadcasted_iota(jnp.int32, values.shape, axis)
+    return jnp.where((index & bit) != 0, pltpu.roll(values, bit, axis), pltpu.roll(values, size - bit, axis))
+
+
+def last_points(band, fine):
+    product = lax.dot_general(fine[...], band, (((1,), (1,)), ((), ())), preferred_element_type=F32)
+    halves = []
+    for half in range(2):
+        values = product[:, 128 * half : 128 * half + 128].reshape(32, 8, 128)
+        row = lax.broadcasted_iota(jnp.int32, values.shape, 1)
+        block = lax.broadcasted_iota(jnp.int32, values.shape, 2) // 16
+        for bit in (1, 2, 4):
+            traded = exchange_bit(exchange_bit(values, 1, bit), 2, 16 * bit)
+            values = jnp.where(((row ^ block) & bit) == 0, values, traded)
+        halves.append(values.reshape(256, 128))
+    return jnp.concatenate(halves, 1)
 
 
 def contrast(labels, values, base, factor):
@@ -134,20 +147,20 @@
     slab = lax.axis_index("slab")
     works_y = (pencil < 24) & (pencil % 2 == 0)
     unit_y = pencil // 4 * 2 + pencil % 4 // 2
-    works_z = lax.rem(slab + 4, SLAB) < UNITS
+    works_z = wrap(slab + 4, SLAB) < UNITS
 
     barrier = pltpu.get_barrier_semaphore()
 
     @pl.when(works_y)
     def _():
         for step in far_first(8, 4)[:-1]:
-            other = lax.rem(pencil + step, PENCIL)
+            other = wrap(pencil + step, PENCIL)
             pl.semaphore_signal(barrier, inc=1, device_id=(other, slab), device_id_type=MESH)
 
     @pl.when(works_z)
     def _():
         for step in far_first(8, 2)[:-1]:
-            other = lax.rem(slab + step, SLAB)
+            other = wrap(slab + step, SLAB)
             pl.semaphore_signal(barrier, inc=1, device_id=(pencil, other), device_id_type=MESH)
 
     moduli_load = pltpu.make_async_copy(moduli_hbm, moduli, in_sems.at[2])
@@ -273,17 +286,20 @@
                 device_id_type=MESH,
             ).start()
 
-    stays = z_place(unit_y, pencil) == slab
+    stays = works_z & (z_unit(slab, pencil) == unit_y)
 
     @pl.when(works_y)
     def _():
         table_loads[2].wait()
         pltpu.make_async_copy(land1, land1, land_sems.at[0]).wait()
-        for chunk in range(4):
-            rows = slice(256 * chunk, 256 * chunk + 256)
+        for begin, end in ((0, 4), (4, 8), (8, 16), (16, 24), (24, 32)):
+            rows = slice(32 * begin, 32 * end)
             band = jnp.dot(along_y[rows, :], land1[...], preferred_element_type=F32)
             send2[rows, :] = (band * (1 / math.sqrt(NY))).astype(BF16)
-            for owner in range(8 * chunk, 8 * chunk + 8):
+            for owner in range(begin, end):
+                if owner % 2 or owner >= 2 * UNITS:
+                    exchange_2(owner, False)
+                    continue
                 own = stays & (pencil == owner)
 
                 @pl.when(own)
@@ -306,34 +322,29 @@
         unit = z_unit(slab, pencil)
         pltpu.make_async_copy(land2, land2, land_sems.at[1]).wait()
         band = transform_z(land2[...], coarse[...], turn)
-        blocks = [band[16 * k : 16 * k + 16] for k in range(16)]
-        turned = [
-            jnp.concatenate([blocks[8 * (k // 8) + (k - delta) % 8] for k in range(16)], 0) for delta in range(8)
-        ]
-        for chunk in range(2):
-            points = last_points(turned, fine, 128 * chunk, 128)
-            for place, owner in enumerate(SLAB_ORDER[8 * chunk : 8 * chunk + 8]):
-                for part in range(2):
-                    row, start = 16 * place + 8 * part, 32 * owner + 16 * part
-                    halves = [points[row : row + 8, 128 * half : 128 * half + 128] for half in range(2)]
-                    send3[start : start + 16, :] = jnp.concatenate(halves, 0).astype(BF16)
-            for owner in SLAB_ORDER[8 * chunk : 8 * chunk + 8]:
-                source, target = send3.at[tile(owner)], land3.at[tile(unit)]
-
-                @pl.when(slab == owner)
-                def _():
-                    pltpu.make_async_copy(source, target, land_sems.at[2]).start()
-
-                @pl.when(slab != owner)
-                def _():
-                    pltpu.make_async_remote_copy(
-                        src_ref=source,
-                        dst_ref=target,
-                        send_sem=send_sems.at[2],
-                        recv_sem=land_sems.at[2],
-                        device_id=(pencil, owner),
-                        device_id_type=MESH,
-                    ).start()
+        points = last_points(band, fine)
+        for place, owner in enumerate(SLAB_ORDER):
+            for part in range(2):
+                row, start = 16 * place + 8 * part, 32 * owner + 16 * part
+                halves = [points[row : row + 8, 128 * half : 128 * half + 128] for half in range(2)]
+                send3[start : start + 16, :] = jnp.concatenate(halves, 0).astype(BF16)
+        for owner in SLAB_ORDER:
+            source, target = send3.at[tile(owner)], land3.at[tile(unit)]
+
+            @pl.when(slab == owner)
+            def _():
+                pltpu.make_async_copy(source, target, land_sems.at[2]).start()
+
+            @pl.when(slab != owner)
+            def _():
+                pltpu.make_async_remote_copy(
+                    src_ref=source,
+                    dst_ref=target,
+                    send_sem=send_sems.at[2],
+                    recv_sem=land_sems.at[2],
+                    device_id=(pencil, owner),
+                    device_id_type=MESH,
+                ).start()
 
     factor = (lam0 + mu0) / (mu0 * (lam0 + 2.0 * mu0))
     half_mu = 1.0 / (2.0 * mu0)
@@ -407,7 +418,7 @@
             pltpu.VMEM((2 * NY, 2 * NY), BF16),
             pltpu.VMEM((512, 512), BF16),
             pltpu.VMEM((2, 16, 128), F32),
-            pltpu.VMEM((8, 256, 256), BF16),
+            pltpu.VMEM((256, 256), BF16),
             pltpu.VMEM((2, 16, 128), F32),
             pltpu.VMEM((2, 8, 128), F32),
             pltpu.VMEM((XW, 16, 128), F32),

time: 35.5 us -> 35 us (0.986)
  no operation moved by 1% of the time
where the time goes in v4:
time: 35 us; the launch traced here: 34.9 us
  Pallas kernels  34.2 us (98%)
  local copies, waits for them, and re-layouts  0.68 us (2%)
    pallas_call x1, Pallas kernels, per_device(): pl.pallas_call(kernel, out_shape=jax.ShapeDtypeStruct((COMPS, 2, MODES, 1...  34.2 us

profile of v4, /device:TPU:1, one launch (start us, length us, event | category | flops | bytes accessed | tf_op | source)
XLA Modules:
  0.0 34.9 jit_solution(1456651191915496611)
XLA Ops:
  0.0 34.2 %shard_map.91 = f32[6,2,2,16,128]{4,3,2,1,0:T(8,128)S(1)} custom-call(f32[2,4]{1,0:T(2,128)} %moduli_hbm.1, bf16[6,16,16,128]{3,2,1,0:T(8,128)(2,1)} %strain_hbm.1, s32[16,16,128]{2,1,0:T(8,128)} %labels_hbm.1, bf16[1024,1024]{1,0:T(8,128)(2,1)} %constant.12.clone.along_y_hbm, bf16[512,512]{1,0:T(8,128)(2,1)} %constant.13.clone.coarse_hbm, ...), custom_call_target="tpu_custom_call" | custom-call | tf_op jit(solution)/shard_map/pallas_call | solution.py:409
  34.2 0.7 %copy.11 = f32[6,2,2,16,128]{4,3,2,1,0:T(8,128)} copy(f32[6,2,2,16,128]{4,3,2,1,0:T(8,128)S(1)} %shard_map.91) | data formatting | bytes 393216

commit v5 on v4

--- a/solution.py
+++ b/solution.py
@@ -13,6 +13,7 @@
 XW, MODES, KX0, NPHASE, COMPS = 16, 2, 64, 4, 6
 PENCIL, SLAB = 32, 16
 UNITS = 12
+Y_PLACES = (0, 2, 5, 7, 8, 10, 13, 15, 16, 18, 21, 23)
 SLAB_ORDER = (0, 1, 2, 3, 14, 15, 4, 5, 12, 13, 6, 7, 10, 11, 8, 9)
 Q_FLOOR = 0.01
 F32, BF16 = jnp.float32, jnp.bfloat16
@@ -145,8 +146,8 @@
 ):
     pencil = lax.axis_index("pencil")
     slab = lax.axis_index("slab")
-    works_y = (pencil < 24) & (pencil % 2 == 0)
-    unit_y = pencil // 4 * 2 + pencil % 4 // 2
+    unit_y = sum(jnp.where(pencil == place, unit, 0) for unit, place in enumerate(Y_PLACES))
+    works_y = sum(jnp.where(pencil == place, 1, 0) for place in Y_PLACES) > 0
     works_z = wrap(slab + 4, SLAB) < UNITS
 
     barrier = pltpu.get_barrier_semaphore()
@@ -246,8 +247,8 @@
     def tile(index):
         return pl.ds(pl.multiple_of(index * 32, 32), 32)
 
-    for unit in (10, 11, 8, 9, 6, 7, 4, 5, 2, 3, 0, 1):
-        place = 4 * (unit // 2) + 2 * (unit % 2)
+    for unit in reversed(range(UNITS)):
+        place = Y_PLACES[unit]
 
         @pl.when(pencil != place)
         def _():
@@ -297,7 +298,7 @@
             band = jnp.dot(along_y[rows, :], land1[...], preferred_element_type=F32)
             send2[rows, :] = (band * (1 / math.sqrt(NY))).astype(BF16)
             for owner in range(begin, end):
-                if owner % 2 or owner >= 2 * UNITS:
+                if owner not in Y_PLACES:
                     exchange_2(owner, False)
                     continue
                 own = stays & (pencil == owner)

time: 35 us -> 34.7 us (level)
  no operation moved by 1% of the time
where the time goes in v5:
time: 34.7 us; the launch traced here: 34.6 us
  Pallas kernels  33.9 us (98%)
  local copies, waits for them, and re-layouts  0.68 us (2%)
    pallas_call x1, Pallas kernels, per_device(): pl.pallas_call(kernel, out_shape=jax.ShapeDtypeStruct((COMPS, 2, MODES, 1...  33.9 us

profile of v5, /device:TPU:1, one launch (start us, length us, event | category | flops | bytes accessed | tf_op | source)
XLA Modules:
  0.0 34.6 jit_solution(12694619080338005372)
XLA Ops:
  0.0 33.9 %shard_map.91 = f32[6,2,2,16,128]{4,3,2,1,0:T(8,128)S(1)} custom-call(f32[2,4]{1,0:T(2,128)} %moduli_hbm.1, bf16[6,16,16,128]{3,2,1,0:T(8,128)(2,1)} %strain_hbm.1, s32[16,16,128]{2,1,0:T(8,128)} %labels_hbm.1, bf16[1024,1024]{1,0:T(8,128)(2,1)} %constant.12.clone.along_y_hbm, bf16[512,512]{1,0:T(8,128)(2,1)} %constant.13.clone.coarse_hbm, ...), custom_call_target="tpu_custom_call" | custom-call | tf_op jit(solution)/shard_map/pallas_call | solution.py:410
  34.0 0.7 %copy.11 = f32[6,2,2,16,128]{4,3,2,1,0:T(8,128)} copy(f32[6,2,2,16,128]{4,3,2,1,0:T(8,128)S(1)} %shard_map.91) | data formatting | bytes 393216

commit v6 on v5

--- a/solution.py
+++ b/solution.py
@@ -13,8 +13,8 @@
 XW, MODES, KX0, NPHASE, COMPS = 16, 2, 64, 4, 6
 PENCIL, SLAB = 32, 16
 UNITS = 12
-Y_PLACES = (0, 2, 5, 7, 8, 10, 13, 15, 16, 18, 21, 23)
-SLAB_ORDER = (0, 1, 2, 3, 14, 15, 4, 5, 12, 13, 6, 7, 10, 11, 8, 9)
+Y_PLACES = (0, 2, 5, 7, 8, 10, 13, 15, 24, 26, 29, 31)
+SLAB_ORDER = (0, 1, 2, 3, 4, 5, 14, 15, 6, 7, 12, 13, 8, 9, 10, 11)
 Q_FLOOR = 0.01
 F32, BF16 = jnp.float32, jnp.bfloat16
 
@@ -46,7 +46,7 @@
     along_y = parts_table(angle).reshape(2, PENCIL, 16, 2, PENCIL, 16)
     along_y = along_y.transpose(1, 0, 2, 4, 3, 5).reshape(2 * NY, 2 * NY)
     angle = 2 * math.pi / 16 * (np.outer(np.arange(16), np.arange(16)) % 16)
-    coarse = np.einsum("obrs,kj->okbsrj", parts_table(angle), np.eye(16)).reshape(512, 512)
+    coarse = np.einsum("obrs,kj->okbsrj", np.roll(parts_table(angle), 4, 3), np.eye(16)).reshape(512, 512)
     angle = 2 * math.pi / NZ * np.outer(np.arange(16), np.arange(128))
     turn = np.stack([np.cos(angle), np.sin(angle)]) / math.sqrt(NZ)
     angle = 2 * math.pi / 128 * (np.outer(np.arange(128), np.arange(128)) % 128)
@@ -68,8 +68,8 @@
     )
 
 
-def transform_z(data, coarse, turn):
-    mixed = jnp.dot(coarse, data, preferred_element_type=F32).reshape(2, 16, 16, 128)
+def turn_z(mixed, turn):
+    mixed = mixed.reshape(2, 16, 16, 128)
     cosine, sine = turn[0][None], turn[1][None]
     real = mixed[0] * cosine + mixed[1] * sine
     imag = mixed[1] * cosine - mixed[0] * sine
@@ -152,17 +152,17 @@
 
     barrier = pltpu.get_barrier_semaphore()
 
+    @pl.when(works_z)
+    def _():
+        for step in far_first(8, 2)[:-1]:
+            other = wrap(slab + step, SLAB)
+            pl.semaphore_signal(barrier, inc=1, device_id=(pencil, other), device_id_type=MESH)
+
     @pl.when(works_y)
     def _():
         for step in far_first(8, 4)[:-1]:
             other = wrap(pencil + step, PENCIL)
             pl.semaphore_signal(barrier, inc=1, device_id=(other, slab), device_id_type=MESH)
-
-    @pl.when(works_z)
-    def _():
-        for step in far_first(8, 2)[:-1]:
-            other = wrap(slab + step, SLAB)
-            pl.semaphore_signal(barrier, inc=1, device_id=(pencil, other), device_id_type=MESH)
 
     moduli_load = pltpu.make_async_copy(moduli_hbm, moduli, in_sems.at[2])
     moduli_load.start()
@@ -271,18 +271,20 @@
     sin_z, cos_z = (jnp.tile(freq_z[i], (2, 1)) for i in range(2))
     cos_yz, sin_cos, cos_sin = cos_y * cos_z, sin_y * cos_z, cos_y * sin_z
 
+    arrival = jnp.where(wrap(slab + 4, SLAB) < SLAB // 2, 1, 3)
+
     def exchange_2(owner, own):
         mine = z_place(unit_y, owner)
         source = send2.at[tile(owner)]
-        target = land2.at[tile(slab)]
+        target = land2.at[tile(wrap(slab + 4, SLAB))]
         if own:
-            pltpu.make_async_copy(source, target, land_sems.at[1]).start()
+            pltpu.make_async_copy(source, target, land_sems.at[arrival]).start()
         else:
             pltpu.make_async_remote_copy(
                 src_ref=source,
                 dst_ref=target,
                 send_sem=send_sems.at[1],
-                recv_sem=land_sems.at[1],
+                recv_sem=land_sems.at[arrival],
                 device_id=(owner, mine),
                 device_id_type=MESH,
             ).start()
@@ -321,8 +323,12 @@
     @pl.when(works_z)
     def _():
         unit = z_unit(slab, pencil)
-        pltpu.make_async_copy(land2, land2, land_sems.at[1]).wait()
-        band = transform_z(land2[...], coarse[...], turn)
+        mixed = None
+        for slabs, arrived in ((slice(0, 256), 1), (slice(256, 512), 3)):
+            pltpu.make_async_copy(land2.at[slabs], land2.at[slabs], land_sems.at[arrived]).wait()
+            part = jnp.dot(coarse[:, slabs], land2[slabs, :], preferred_element_type=F32)
+            mixed = part if mixed is None else mixed + part
+        band = turn_z(mixed, turn)
         points = last_points(band, fine)
         for place, owner in enumerate(SLAB_ORDER):
             for part in range(2):
@@ -432,7 +438,7 @@
             pltpu.SemaphoreType.DMA((3,)),
             pltpu.SemaphoreType.DMA((6,)),
             pltpu.SemaphoreType.DMA((3,)),
-            pltpu.SemaphoreType.DMA((3,)),
+            pltpu.SemaphoreType.DMA((4,)),
         ],
         compiler_params=pltpu.CompilerParams(
             collective_id=0, has_side_effects=True, vmem_limit_bytes=32 * 1024 * 1024

time: 34.7 us -> 33.8 us (0.974)
  Pallas kernels: 33.9 us -> 33 us
    pallas_call x1, Pallas kernels: 33.9 us -> 33 us  [per_device(): pl.pallas_call(kernel, out_shape=jax.ShapeDtypeStruct((COMPS, 2, MODES, 1...]
where the time goes in v6:
time: 33.8 us; the launch traced here: 33.7 us
  Pallas kernels  33 us (98%)
  local copies, waits for them, and re-layouts  0.68 us (2%)
    pallas_call x1, Pallas kernels, per_device(): pl.pallas_call(kernel, out_shape=jax.ShapeDtypeStruct((COMPS, 2, MODES, 1...  33 us
    unnamed x1, local copies, waits for them, and re-layouts  0.68 us

profile of v6, /device:TPU:1, one launch (start us, length us, event | category | flops | bytes accessed | tf_op | source)
XLA Modules:
  0.0 33.7 jit_solution(718383602226812841)
XLA Ops:
  0.0 33.0 %shard_map.91 = f32[6,2,2,16,128]{4,3,2,1,0:T(8,128)S(1)} custom-call(f32[2,4]{1,0:T(2,128)} %moduli_hbm.1, bf16[6,16,16,128]{3,2,1,0:T(8,128)(2,1)} %strain_hbm.1, s32[16,16,128]{2,1,0:T(8,128)} %labels_hbm.1, bf16[1024,1024]{1,0:T(8,128)(2,1)} %constant.12.clone.along_y_hbm, bf16[512,512]{1,0:T(8,128)(2,1)} %constant.13.clone.coarse_hbm, ...), custom_call_target="tpu_custom_call" | custom-call | tf_op jit(solution)/shard_map/pallas_call | solution.py:416
  33.0 0.7 %copy.11 = f32[6,2,2,16,128]{4,3,2,1,0:T(8,128)} copy(f32[6,2,2,16,128]{4,3,2,1,0:T(8,128)S(1)} %shard_map.91) | data formatting | bytes 393216

commit v7 on v6

--- a/solution.py
+++ b/solution.py
@@ -247,7 +247,7 @@
     def tile(index):
         return pl.ds(pl.multiple_of(index * 32, 32), 32)
 
-    for unit in reversed(range(UNITS)):
+    for unit in (7, 6, 11, 10, 5, 4, 9, 8, 3, 2, 1, 0):
         place = Y_PLACES[unit]
 
         @pl.when(pencil != place)

time: 33.8 us -> 33.9 us (level)
  no operation moved by 1% of the time
where the time goes in v7:
time: 33.9 us; the launch traced here: 33.8 us
  Pallas kernels  33.1 us (98%)
  local copies, waits for them, and re-layouts  0.68 us (2%)
    pallas_call x1, Pallas kernels, per_device(): pl.pallas_call(kernel, out_shape=jax.ShapeDtypeStruct((COMPS, 2, MODES, 1...  33.1 us
    unnamed x1, local copies, waits for them, and re-layouts  0.68 us

profile of v7, /device:TPU:1, one launch (start us, length us, event | category | flops | bytes accessed | tf_op | source)
XLA Modules:
  0.0 33.8 jit_solution(5904203367169591588)
XLA Ops:
  0.0 33.1 %shard_map.91 = f32[6,2,2,16,128]{4,3,2,1,0:T(8,128)S(1)} custom-call(f32[2,4]{1,0:T(2,128)} %moduli_hbm.1, bf16[6,16,16,128]{3,2,1,0:T(8,128)(2,1)} %strain_hbm.1, s32[16,16,128]{2,1,0:T(8,128)} %labels_hbm.1, bf16[1024,1024]{1,0:T(8,128)(2,1)} %constant.12.clone.along_y_hbm, bf16[512,512]{1,0:T(8,128)(2,1)} %constant.13.clone.coarse_hbm, ...), custom_call_target="tpu_custom_call" | custom-call | tf_op jit(solution)/shard_map/pallas_call | solution.py:416
  33.1 0.7 %copy.11 = f32[6,2,2,16,128]{4,3,2,1,0:T(8,128)} copy(f32[6,2,2,16,128]{4,3,2,1,0:T(8,128)S(1)} %shard_map.91) | data formatting | bytes 393216
